TPU v7x, 256 devices: a whole 4x4x8 slice. The times are simulated.
256 devices in a mesh: dp: 4 (over z_lo), ctx: 64 (over z_hi, y, x, core).
Axes of the slice: x: 4, y: 4, z: 8 (z_hi: 2, z_lo: 4; z = z_hi * 4 + z_lo), core: 2. Of those that a mesh axis runs over, the one named last changes fastest.
Arguments:
- qkv: bfloat16 [4, 8192, 6144], P('dp', 'ctx'), may hold values from -6 to 6
- short_filter: float32 [7, 768], replicated, may hold values from -2 to 2
- long_filter: float32 [2048, 8192], P('ctx'), may hold values from -1.1 to 1.1
- cotangent: bfloat16 [4, 8192, 2048], P('dp', 'ctx'), may hold values from -6 to 6
Outputs:
- mixer_out: bfloat16 [4, 8192, 2048], P('dp', 'ctx')
- grad_qkv: bfloat16 [4, 8192, 6144], P('dp', 'ctx')
- grad_long: float32 [2048, 8192], P('ctx')
- grad_short: float32 [7, 768], replicated
All inputs are finite; a program needn't handle non-finite values.
Results may differ from a plain program's by a relative error of at most 0.014.
Values may be sent and summed in bfloat16 or wider, within the bound.
No kernel may reach another device: no remote copies, remote signals or barrier semaphores. Data moves between devices by JAX's collectives and lax.ppermute only.
A program may use at most 128 MiB of HBM per device.

v0:
```python
import math
import jax
import jax.numpy as jnp
from jax import lax
from jax.sharding import PartitionSpec as P

precise = lax.Precision.HIGHEST


def from_behind(array, axis, by):
    devices = lax.axis_size(axis)
    pairs = [(i, i + by) for i in range(devices) if 0 <= i + by < devices]
    return lax.ppermute(array, axis, pairs)


def angles(row_count, col_count, period):
    row_iota = lax.broadcasted_iota(jnp.int32, (row_count, col_count), 0)
    col_iota = lax.broadcasted_iota(jnp.int32, (row_count, col_count), 1)
    return (row_iota * col_iota % period).astype(jnp.float32) * (2.0 * math.pi / period)


def matmul(left_side, right_side):
    return jnp.dot(left_side, right_side, precision=precise, preferred_element_type=jnp.float32)


def column_table(col_count, sign_flip):
    angle_cols = angles(col_count, col_count, col_count)
    cos_part = jnp.cos(angle_cols)
    sin_part = sign_flip * jnp.sin(angle_cols)
    upper = jnp.concatenate([cos_part, sin_part], axis=1)
    lower = jnp.concatenate([-sin_part, cos_part], axis=1)
    return jnp.concatenate([upper, lower], axis=0)


def forward_transform(signal):
    half_rows, own_chans, col_count = signal.shape
    row_count = 2 * half_rows
    total_len = row_count * col_count
    angle_rows = angles(row_count, half_rows, row_count)
    row_table = jnp.concatenate([jnp.cos(angle_rows), -jnp.sin(angle_rows)], axis=0)
    rows_out = matmul(
        row_table, signal.reshape(half_rows, own_chans * col_count).astype(jnp.float32)
    )
    rows_out = rows_out.reshape(2, row_count, own_chans, col_count)
    part_real = rows_out[0]
    part_imag = rows_out[1]
    twist = angles(row_count, col_count, total_len)[:, None, :]
    twist_real = jnp.cos(twist)
    twist_imag = -jnp.sin(twist)
    turned = jnp.concatenate(
        [
            part_real * twist_real - part_imag * twist_imag,
            part_real * twist_imag + part_imag * twist_real,
        ],
        axis=2,
    )
    spec = matmul(
        turned.reshape(row_count * own_chans, 2 * col_count), column_table(col_count, -1.0)
    )
    return spec.reshape(row_count, own_chans, 2 * col_count)


def inverse_transform(spec):
    row_count, own_chans, double_cols = spec.shape
    col_count = double_cols // 2
    half_rows = row_count // 2
    total_len = row_count * col_count
    back = matmul(spec.reshape(row_count * own_chans, double_cols), column_table(col_count, 1.0))
    back = back.reshape(row_count, own_chans, double_cols)
    back_real = back[:, :, :col_count]
    back_imag = back[:, :, col_count:]
    twist = angles(row_count, col_count, total_len)[:, None, :]
    twist_real = jnp.cos(twist)
    twist_imag = jnp.sin(twist)
    turned = jnp.concatenate(
        [
            back_real * twist_real - back_imag * twist_imag,
            back_real * twist_imag + back_imag * twist_real,
        ],
        axis=0,
    )
    angle_rows = angles(half_rows, row_count, row_count)
    row_table = jnp.concatenate([jnp.cos(angle_rows), -jnp.sin(angle_rows)], axis=1) * (
        1.0 / total_len
    )
    result = matmul(row_table, turned.reshape(2 * row_count, own_chans * col_count))
    return result.reshape(half_rows, own_chans, col_count)


def spec_times(first_spec, second_spec, conjugate):
    col_count = first_spec.shape[2] // 2
    first_real = first_spec[:, :, :col_count]
    first_imag = first_spec[:, :, col_count:]
    second_real = second_spec[:, :, :col_count]
    second_imag = conjugate * second_spec[:, :, col_count:]
    return jnp.concatenate(
        [
            first_real * second_real - first_imag * second_imag,
            first_real * second_imag + first_imag * second_real,
        ],
        axis=2,
    )


def shards(qkv, short_filter, long_filter, cotangent):
    seq_rows = qkv[0]
    row_count, width_all = seq_rows.shape
    width = width_all // 3
    tap_count = short_filter.shape[0]
    group_size = width_all // short_filter.shape[1]
    ctx_count = lax.axis_size("ctx")
    own_chans = width // ctx_count
    grad_scale = 1.0 / math.sqrt(lax.axis_size("dp") * ctx_count * row_count)
    tap_weights = jnp.repeat(short_filter, group_size, axis=1)
    left_rim = from_behind(seq_rows[row_count - tap_count + 1 :], "ctx", 1)
    padded = jnp.concatenate([left_rim, seq_rows], axis=0).astype(jnp.float32)
    short_out = jnp.zeros((row_count, width_all), jnp.float32)
    for lag_index in range(tap_count):
        start = tap_count - 1 - lag_index
        short_out = short_out + tap_weights[lag_index] * padded[start : start + row_count]
    query_rows = short_out[:, :width]
    key_rows = short_out[:, width : 2 * width]
    value_rows = short_out[:, 2 * width :]
    cot_rows = cotangent[0].astype(jnp.float32)
    product = (key_rows * value_rows).T.astype(jnp.bfloat16)[None]
    grad_out = (cot_rows * query_rows).T.astype(jnp.bfloat16)[None]
    filter_taps = long_filter.reshape(own_chans, ctx_count, row_count).transpose(1, 0, 2)
    filter_spec = forward_transform(filter_taps)
    own_prod = lax.all_to_all(product, "ctx", split_axis=1, concat_axis=0, tiled=True)
    prod_spec = forward_transform(own_prod)
    y_own = inverse_transform(spec_times(prod_spec, filter_spec, 1.0))
    y_own, prod_spec = (y_own.astype(jnp.bfloat16), prod_spec)
    long_back = lax.all_to_all(y_own, "ctx", split_axis=0, concat_axis=1, tiled=True)
    own_grad = lax.all_to_all(grad_out, "ctx", split_axis=1, concat_axis=0, tiled=True)
    grad_spec = forward_transform(own_grad)
    du_own = inverse_transform(spec_times(grad_spec, filter_spec, -1.0))
    dh_own = inverse_transform(spec_times(grad_spec, prod_spec, -1.0))
    du_own, dh_own = (du_own.astype(jnp.bfloat16), dh_own)
    du_back = lax.all_to_all(du_own, "ctx", split_axis=0, concat_axis=1, tiled=True)
    long_rows = long_back[0].T.astype(jnp.float32)
    mixer_out = (query_rows * long_rows).astype(jnp.bfloat16)[None]
    grad_prod = du_back[0].T.astype(jnp.float32)
    grad_short_out = jnp.concatenate(
        [cot_rows * long_rows, grad_prod * value_rows, grad_prod * key_rows], axis=1
    )
    right_rim = from_behind(grad_short_out[: tap_count - 1].astype(jnp.bfloat16), "ctx", -1).astype(
        jnp.float32
    )
    grad_padded = jnp.concatenate([grad_short_out, right_rim], axis=0)
    grad_rows = jnp.zeros((row_count, width_all), jnp.float32)
    for lag_index in range(tap_count):
        grad_rows = (
            grad_rows + tap_weights[lag_index] * grad_padded[lag_index : lag_index + row_count]
        )
    grad_qkv = grad_rows.astype(jnp.bfloat16)[None]
    lag_terms = []
    for lag_index in range(tap_count):
        start = tap_count - 1 - lag_index
        lag_terms.append(jnp.sum(grad_short_out * padded[start : start + row_count], axis=0))
    short_terms = jnp.stack(lag_terms).reshape(tap_count, -1, group_size).sum(axis=2) * grad_scale
    long_terms = dh_own.transpose(1, 0, 2).reshape(own_chans, ctx_count * row_count) * grad_scale
    grad_short = lax.psum(short_terms, ("dp", "ctx"))
    grad_long = lax.psum(long_terms.astype(jnp.bfloat16), "dp").astype(jnp.float32)
    return (mixer_out, grad_qkv, grad_long, grad_short)


def solution(mesh):
    return jax.shard_map(
        shards,
        mesh=mesh,
        in_specs=(P("dp", "ctx", None), P(), P("ctx", None), P("dp", "ctx", None)),
        out_specs=(P("dp", "ctx", None), P("dp", "ctx", None), P("ctx", None), P()),
        check_vma=False,
    )
```

profile of v0, /device:TPU:1, one launch (start us, length us, event | category | flops | bytes accessed | tf_op | source)
XLA Modules:
  0.0 534.2 jit_solution(974061488572454364)
XLA Ops:
  8.2 4.5 collective-permute-start
  15.1 5.7 %fusion.53 = f32[256,4096]{1,0:T(8,128)} fusion(f32[8,8,32,128]{3,2,1,0:T(8,128)S(1)} %bitcast.145, f32[128,64]{1,0:T(8,128)S(1)} %get-tuple-element.64, f32[128,64]{1,0:T(8,128)S(1)} %get-tuple-element.65), kind=kOutput, calls=%fused_computation.90 | convolution fusion | flops 805322752 | bytes 5308416 | tf_op jit(solution)/shard_map/dot_general | solution.py:23
  28.0 11.8 %multiply_add_fusion = f32[128,6144]{0,1:T(8,128)S(1)} fusion(f32[134,6144]{0,1:T(8,128)S(1)} %maximum_convert_fusion, f32[6144]{0:T(1024)S(1)} %broadcast_in_dim.60, f32[6144]{0:T(1024)S(1)} %broadcast_in_dim.58, f32[6144]{0:T(1024)S(1)} %broadcast_in_dim.56, f32[6144]{0:T(1024)S(1)} %broadcast_in_dim.54, f32[6144]{0:T(1024)S(1)} %broadcast_in_dim.52, ...), kind=kLoop, calls=%fused_computation.57 | loop fusion | flops 10223616 | bytes 25337856 | tf_op jit(solution)/shard_map/add | solution.py:120
  41.6 8.1 %copy.95 = bf16[1,2048,128]{2,0,1:T(2,128)(2,1)S(1)} copy(bf16[1,2048,128]{2,1,0:T(8,128)(2,1)S(1)} %fusion.62) | data formatting | bytes 1048576 | tf_op jit(solution)/shard_map/broadcast_in_dim | solution.py:126
  50.2 12.0 %reduce.18 = bf16[2048,128]{1,0:T(8,128)(2,1)S(1)} reduce(bf16[2048,1,128]{2,1,0:T(2,128)(2,1)S(1)} %bitcast.143, bf16[]{:T(256)} %broadcast.244), dimensions={1}, to_apply=%bitcast.134.reduce_sub_computation | reduce | bytes 1048578
  63.1 14.1 %all-to-all-start.2 = ((bf16[64,2,2048]{2,1,0:T(2,128)(2,1)}), bf16[64,2,2048]{2,1,0:T(2,128)(2,1)}, u32[]{:S(2)}, u32[]{:S(2)}) async-start(bf16[64,2,2048]{2,1,0:T(2,128)(2,1)} %reshape.246), calls=%async_computation.2 | async-start | bytes 1048576 | tf_op jit(solution)/shard_map/all_to_all | solution.py:134
  77.3 4.7 fusion.130
  94.4 3.6 reshape.247
  98.1 8.8 %bitcast_reduce_fusion.1 = bf16[2048,128]{1,0:T(8,128)(2,1)S(1)} fusion(bf16[2048,1,128]{2,1,0:T(2,128)(2,1)S(1)} %reshape.247), kind=kLoop, calls=%fused_computation.202 | loop fusion | bytes 1048576 | tf_op jit(solution)/shard_map/all_to_all | solution.py:134
  118.9 4.7 multiply_subtract_fusion.4
  133.0 3.9 fusion.16
  139.9 5.6 %copy.63 = f32[256,32,128]{0,2,1:T(8,128)} copy(f32[256,32,128]{2,0,1:T(8,128)} %pad_maximum_fusion.2) | data formatting | bytes 8388608 | tf_op jit(solution)/shard_map/concatenate | solution.py:75
  145.5 6.4 %fusion.49 = bf16[64,32,128]{2,0,1:T(8,128)(2,1)S(1)} fusion(f32[256,32,128]{0,2,1:T(8,128)} %copy.63, f32[64,128]{1,0:T(8,128)S(1)} %copy-done.20, f32[64,128]{1,0:T(8,128)S(1)} %copy-done.22), kind=kOutput, calls=%fused_computation.88 | convolution fusion | flops 805601280 | bytes 4784128 | tf_op jit(solution)/shard_map/dot_general | solution.py:23
  152.3 29.5 %all_to_all.16 = bf16[64,32,128]{2,1,0:T(8,128)(2,1)S(1)} all-to-all(bf16[64,32,128]{2,1,0:T(8,128)(2,1)S(1)} %copy.64), channel_id=1, replica_groups=mesh['dp'=4,'ctx'=64] {'ctx'}, dimensions={0} | all-to-all | bytes 1048576 | tf_op jit(solution)/shard_map/all_to_all | solution.py:139
  182.0 8.1 %copy.96 = bf16[1,2048,128]{2,0,1:T(2,128)(2,1)S(1)} copy(bf16[1,2048,128]{2,1,0:T(8,128)(2,1)S(1)} %get-tuple-element.57) | data formatting | bytes 1048576 | tf_op jit(solution)/shard_map/broadcast_in_dim | solution.py:125
  190.2 12.3 %reduce.19 = bf16[2048,128]{1,0:T(8,128)(2,1)} reduce(bf16[2048,1,128]{2,1,0:T(2,128)(2,1)S(1)} %bitcast.144, bf16[]{:T(256)} %broadcast.244), dimensions={1}, to_apply=%bitcast.135.reduce_sub_computation | reduce | bytes 1048578
  203.7 21.0 %all_to_all.17 = bf16[64,2,2048]{2,1,0:T(2,128)(2,1)} all-to-all(bf16[64,2,2048]{2,1,0:T(2,128)(2,1)S(1)} %reshape.248), channel_id=1, replica_groups=mesh['dp'=4,'ctx'=64] {'ctx'}, dimensions={0} | all-to-all | bytes 1048576 | tf_op jit(solution)/shard_map/all_to_all | solution.py:129
  228.3 9.6 %bitcast_reduce_fusion = bf16[2048,128]{1,0:T(8,128)(2,1)} fusion(bf16[2048,1,128]{2,1,0:T(2,128)(2,1)S(1)} %reshape.249), kind=kLoop, calls=%fused_computation.201 | loop fusion | bytes 1048576 | tf_op jit(solution)/shard_map/all_to_all | solution.py:129
  242.6 5.0 fusion
  247.7 6.2 %multiply_subtract_fusion.1 = (f32[128,32,128]{2,0,1:T(8,128)}, f32[128,32,128]{2,0,1:T(8,128)}, f32[128,32,128]{2,0,1:T(8,128)S(1)}, f32[128,32,128]{2,0,1:T(8,128)}) fusion(f32[128,32,256]{2,0,1:T(8,128)S(1)} %copy-done.4, f32[128,32,256]{2,0,1:T(8,128)} %fusion, f32[128,32,256]{2,0,1:T(8,128)S(1)} %copy-done.6), kind=kLoop, calls=%fused_computation.69 | loop fusion | flops 6815744 | bytes 20971520 | tf_op jit(solution)/shard_map/sub | solution.py:98
  253.9 5.7 %fusion.20 = f32[128,32,256]{2,0,1:T(8,128)S(1)} fusion(f32[128,32,128]{2,0,1:T(8,128)} %get-tuple-element.30, f32[128,32,128]{2,0,1:T(8,128)} %get-tuple-element.29, f32[128,128]{1,0:T(8,128)S(1)} %get-tuple-element.69, f32[128,128]{1,0:T(8,128)S(1)} %get-tuple-element.71, f32[128,128]{1,0:T(8,128)S(1)} %get-tuple-element.70), kind=kOutput, calls=%fused_computation.23 | convolution fusion | flops 3222470656 | bytes 8585216 | tf_op jit(solution)/shard_map/dot_general | solution.py:23
  268.5 5.6 %copy.53 = f32[256,32,128]{0,2,1:T(8,128)} copy(f32[256,32,128]{2,0,1:T(8,128)} %pad_maximum_fusion.1) | data formatting | bytes 8388608 | tf_op jit(solution)/shard_map/concatenate | solution.py:75
  274.1 6.2 %fusion.46 = bf16[64,32,128]{2,0,1:T(8,128)(2,1)S(1)} fusion(f32[256,32,128]{0,2,1:T(8,128)} %copy.53, f32[64,128]{1,0:T(8,128)S(1)} %copy-done.21, f32[64,128]{1,0:T(8,128)S(1)} %copy-done.23), kind=kOutput, calls=%fused_computation.87 | convolution fusion | flops 805601280 | bytes 4784128 | tf_op jit(solution)/shard_map/dot_general | solution.py:23
  281.4 9.5 %all-to-all-start.1 = ((bf16[64,32,128]{2,1,0:T(8,128)(2,1)}), bf16[64,32,128]{2,1,0:T(8,128)(2,1)}, u32[]{:S(2)}, u32[]{:S(2)}) async-start(bf16[64,32,128]{2,1,0:T(8,128)(2,1)} %copy.54), calls=%async_computation.1 | async-start | bytes 1048576 | tf_op jit(solution)/shard_map/all_to_all | solution.py:133
  291.0 4.7 pad_maximum_fusion.3
  295.7 6.0 %copy.67 = f32[256,32,128]{0,2,1:T(8,128)} copy(f32[256,32,128]{2,0,1:T(8,128)} %pad_maximum_fusion.3) | data formatting | bytes 8388608 | tf_op jit(solution)/shard_map/concatenate | solution.py:75
  301.7 6.2 %fusion.43 = bf16[64,32,128]{2,0,1:T(8,128)(2,1)S(1)} fusion(f32[256,32,128]{0,2,1:T(8,128)} %copy.67, f32[64,128]{1,0:T(8,128)S(1)} %copy-done.21, f32[64,128]{1,0:T(8,128)S(1)} %copy-done.23), kind=kOutput, calls=%fused_computation.86 | convolution fusion | flops 805863424 | bytes 4784128 | tf_op jit(solution)/shard_map/dot_general | solution.py:23
  309.0 55.1 %all-reduce.2.cloned.1.call-done = bf16[32,8192]{1,0:T(8,128)(2,1)} async-done(((bf16[32,8192]{1,0:T(8,128)(2,1)}), bf16[32,8192]{1,0:T(8,128)(2,1)}) %all-reduce.2.cloned.1.call-update) | async-done | bytes 524304 | tf_op jit(solution)/shard_map/psum | solution.py:163
  368.7 27.9 %multiply_reduce_fusion = (f32[6144]{0:T(1024)}, f32[6144]{0:T(1024)}, f32[6144]{0:T(1024)}, f32[6144]{0:T(1024)}, f32[6144]{0:T(1024)}, /*index=5*/f32[6144]{0:T(1024)}, f32[6144]{0:T(1024)}) fusion(f32[134,6144]{0,1:T(8,128)} %copy-done.2, f32[128,2048]{0,1:T(8,128)S(1)} %get-tuple-element.56, f32[128,2048]{0,1:T(8,128)S(1)} %get-tuple-element.55, ...), kind=kLoop, calls=%fused_computation.50 | loop fusion | flops 12539904 | bytes 25337856 | tf_op jit(solution)/shard_map/reduce_sum | solution.py:159
  413.0 4.6 collective-permute-start.1
  428.7 77.5 %psum.15 = f32[7,768]{1,0:T(8,128)} all-reduce(f32[7,768]{1,0:T(8,128)S(1)} %broadcast_multiply_fusion.1), channel_id=1, replica_groups=mesh['dp'=4,'ctx'=64] {'dp','ctx'}, use_global_device_ids=true, to_apply=%region_9.10 | all-reduce | flops 5376 | bytes 43008 | tf_op jit(solution)/shard_map/psum | solution.py:162
  510.8 13.7 %fusion.39 = bf16[1,128,6144]{1,2,0:T(8,128)(2,1)} fusion(f32[134,6144]{0,1:T(8,128)S(1)} %pad_maximum_fusion, f32[6144]{0:T(1024)S(1)} %copy-done.36, f32[6144]{0:T(1024)S(1)} %copy-done.38, f32[6144]{0:T(1024)S(1)} %copy-done.28, f32[6144]{0:T(1024)S(1)} %copy-done.30, f32[6144]{0:T(1024)S(1)} %copy-done.32, f32[6144]{0:T(1024)S(1)} %copy-done.34, ...), kind=kLoop, calls=%fused_computation.82 | loop fusion | flops 12582912 | bytes 23764992 | tf_op jit(solution)/shard_map/broadcast_in_dim | solution.py:155
  (177 shorter events, 110.7 us)
Async XLA Ops:
  7.2 7.7 %copy-start = (f32[32,8192]{1,0:T(8,128)S(1)}, f32[32,8192]{1,0:T(8,128)}, u32[]{:S(2)}) copy-start(f32[32,8192]{1,0:T(8,128)} %param.6) | copy-start | bytes 3145732
  8.2 15.6 %collective-permute-start = (bf16[6,6144]{1,0:T(8,128)(2,1)S(1)}, bf16[6,6144]{1,0:T(8,128)(2,1)S(1)}, u32[]{:S(2)}, u32[]{:S(2)}) collective-permute-start(bf16[6,6144]{1,0:T(8,128)(2,1)S(1)} %slice_bitcast_fusion.2), channel_id=1, source_target_pairs={{0,1},{1,2},{2,3},{3,4},{4,5},{5,6},{6,7},{7,8},{8,9},{9,10},{10,1... | collective-permute-start | bytes 221192 | tf_op jit(solution)/shard_map/ppermute | solution.py:13
  15.1 5.7 %copy-start.39 = (f32[7,768]{1,0:T(8,128)S(1)}, f32[7,768]{1,0:T(8,128)}, u32[]{:S(2)}) copy-start(f32[7,768]{1,0:T(8,128)} %param.5) | copy-start | bytes 64516
  20.8 2.7 copy-start.24
  21.2 6.8 %copy-start.25 = (f32[6144]{0:T(1024)}, f32[6144]{0:T(1024)S(1)}, u32[]{:S(2)}) copy-start(f32[6144]{0:T(1024)S(1)} %broadcast_in_dim.48) | copy-start | bytes 73732
  21.6 6.4 %copy-start.27 = (f32[6144]{0:T(1024)}, f32[6144]{0:T(1024)S(1)}, u32[]{:S(2)}) copy-start(f32[6144]{0:T(1024)S(1)} %broadcast_in_dim.56) | copy-start | bytes 73732
  22.0 6.0 %copy-start.29 = (f32[6144]{0:T(1024)}, f32[6144]{0:T(1024)S(1)}, u32[]{:S(2)}) copy-start(f32[6144]{0:T(1024)S(1)} %broadcast_in_dim.54) | copy-start | bytes 73732
  22.4 5.6 %copy-start.31 = (f32[6144]{0:T(1024)}, f32[6144]{0:T(1024)S(1)}, u32[]{:S(2)}) copy-start(f32[6144]{0:T(1024)S(1)} %broadcast_in_dim.52) | copy-start | bytes 73732
  22.7 5.3 copy-start.33
  23.1 4.9 copy-start.35
  23.5 4.5 copy-start.37
  23.8 16.1 %copy-start.11 = (bf16[1,128,2048]{1,2,0:T(8,128)(2,1)}, bf16[1,128,2048]{1,2,0:T(8,128)(2,1)S(1)}, u32[]{:S(2)}) copy-start(bf16[1,128,2048]{1,2,0:T(8,128)(2,1)S(1)} %copy.55) | copy-start | bytes 1572868
  28.0 11.9 %copy-start.2 = (f32[134,6144]{0,1:T(8,128)}, f32[134,6144]{0,1:T(8,128)S(1)}, u32[]{:S(2)}) copy-start(f32[134,6144]{0,1:T(8,128)S(1)} %maximum_convert_fusion) | copy-start | bytes 9879556
  63.1 31.3 %all-to-all-start.2 = ((bf16[64,2,2048]{2,1,0:T(2,128)(2,1)}), bf16[64,2,2048]{2,1,0:T(2,128)(2,1)}, u32[]{:S(2)}, u32[]{:S(2)}) async-start(bf16[64,2,2048]{2,1,0:T(2,128)(2,1)} %reshape.246), calls=%async_computation.2 | async-start | bytes 1048576 | tf_op jit(solution)/shard_map/all_to_all | solution.py:134
  118.9 4.7 copy-start.12
  118.9 4.7 copy-start.14
  127.3 3.6 copy-start.3
  133.0 3.9 copy-start.16
  139.9 5.6 %copy-start.20 = (f32[64,128]{1,0:T(8,128)S(1)}, f32[64,128]{1,0:T(8,128)}, u32[]{:S(2)}) copy-start(f32[64,128]{1,0:T(8,128)} %get-tuple-element.72) | copy-start | bytes 98308
  139.9 5.6 %copy-start.22 = (f32[64,128]{1,0:T(8,128)S(1)}, f32[64,128]{1,0:T(8,128)}, u32[]{:S(2)}) copy-start(f32[64,128]{1,0:T(8,128)} %get-tuple-element.73) | copy-start | bytes 98308
  145.5 36.3 %copy-start.9 = (f32[128,6144]{0,1:T(8,128)S(1)}, f32[128,6144]{0,1:T(8,128)}, u32[]{:S(2)}) copy-start(f32[128,6144]{0,1:T(8,128)} %copy-done.8) | copy-start | bytes 9437188
  242.6 5.0 copy-start.4
  242.6 5.0 copy-start.6
  253.9 5.7 %copy-start.10 = (f32[128,32,128]{2,0,1:T(8,128)S(1)}, f32[128,32,128]{2,0,1:T(8,128)}, u32[]{:S(2)}) copy-start(f32[128,32,128]{2,0,1:T(8,128)} %get-tuple-element.48) | copy-start | bytes 6291460
  259.6 3.6 copy-start.17
  268.5 5.6 %copy-start.21 = (f32[64,128]{1,0:T(8,128)S(1)}, f32[64,128]{1,0:T(8,128)}, u32[]{:S(2)}) copy-start(f32[64,128]{1,0:T(8,128)} %get-tuple-element.72) | copy-start | bytes 98308
  268.5 5.6 %copy-start.23 = (f32[64,128]{1,0:T(8,128)S(1)}, f32[64,128]{1,0:T(8,128)}, u32[]{:S(2)}) copy-start(f32[64,128]{1,0:T(8,128)} %get-tuple-element.73) | copy-start | bytes 98308
  281.4 84.8 %all-to-all-start.1 = ((bf16[64,32,128]{2,1,0:T(8,128)(2,1)}), bf16[64,32,128]{2,1,0:T(8,128)(2,1)}, u32[]{:S(2)}, u32[]{:S(2)}) async-start(bf16[64,32,128]{2,1,0:T(8,128)(2,1)} %copy.54), calls=%async_computation.1 | async-start | bytes 1048576 | tf_op jit(solution)/shard_map/all_to_all | solution.py:133
  290.9 73.2 %all-reduce.2.cloned.1.call-start = ((), (), s32[]{:S(2)}) async-start(), calls=%async_computation.4 | async-start | bytes 1048576 | tf_op jit(solution)/shard_map/psum | solution.py:163
  368.7 139.6 %copy-start.7 = (f32[128,2048]{0,1:T(8,128)}, f32[128,2048]{0,1:T(8,128)S(1)}, u32[]{:S(2)}) copy-start(f32[128,2048]{0,1:T(8,128)S(1)} %get-tuple-element.58) | copy-start | bytes 3145732
  413.0 93.2 %collective-permute-start.1 = (bf16[6,6144]{1,0:T(8,128)(2,1)S(1)}, bf16[6,6144]{1,0:T(8,128)(2,1)S(1)}, u32[]{:S(2)}, u32[]{:S(2)}) collective-permute-start(bf16[6,6144]{1,0:T(8,128)(2,1)S(1)} %copy.65), channel_id=1, source_target_pairs={{1,0},{2,1},{3,2},{4,3},{5,4},{6,5},{7,6},{8,7},{9,8},{10,9},{11,1... | collective-permute-start | bytes 221192 | tf_op jit(solution)/shard_map/ppermute | solution.py:13
  510.8 16.3 %copy-start.1 = (f32[32,8192]{1,0:T(8,128)S(1)}, f32[32,8192]{1,0:T(8,128)}, u32[]{:S(2)}) copy-start(f32[32,8192]{1,0:T(8,128)} %param.6) | copy-start | bytes 3145732
  (13 other events, 25.7 us)
Sparse Core Ops, SparseCore 0:
  309.2 54.9 all-reduce.1
where the time goes:
time: 545 us; the launch traced here: 534 us
  local copies, waits for them, and re-layouts  129 us (24%)
  blocking collectives  128 us (23%)
  other arithmetic  120 us (22%)
  waiting for transfers between devices  55.4 us (10%)
  matrix products  53.4 us (10%)
  starting transfers between devices  32.8 us (6%)
  between operations  15.1 us (3%)
    psum x1, blocking collectives, shards(): grad_short = lax.psum(short_terms, ('dp', 'ctx'))  77.5 us
    psum x1, waiting for transfers between devices, shards(): lax.psum(long_terms.astype(jnp.bfloat16), 'dp').astype(jnp.float32)  55.1 us
    dot_general x12, matrix products, matmul(): jnp.dot(left_side, right_side, precision=precise, preferred_element_type=...  53.4 us
    unnamed x97, local copies, waits for them, and re-layouts  30 us
    all_to_all x1, blocking collectives, shards(): lax.all_to_all(du_own, 'ctx', split_axis=0, concat_axis=1, tiled=True)  29.5 us
    reduce_sum x1, other arithmetic, shards(): jnp.sum(grad_short_out * padded[start:start + row_count], axis=0)  27.9 us
    unnamed x2, other arithmetic  24.3 us
    all_to_all x1, blocking collectives, shards(): lax.all_to_all(product, 'ctx', split_axis=1, concat_axis=0, tiled=True)  21 us
  transfers between devices with their start and end apart: 5, of which 2 were waited for; matrix products, arithmetic and copies ran while one was open for 11% of the time, Pallas kernels for 0%

commit v1 on v0

--- a/solution.py
+++ b/solution.py
@@ -136,7 +136,10 @@
     du_own = inverse_transform(spec_times(grad_spec, filter_spec, -1.0))
     dh_own = inverse_transform(spec_times(grad_spec, prod_spec, -1.0))
     du_own, dh_own = (du_own.astype(jnp.bfloat16), dh_own)
-    du_back = lax.all_to_all(du_own, "ctx", split_axis=0, concat_axis=1, tiled=True)
+    du_back = jnp.concatenate(
+        lax.all_to_all(jnp.stack(jnp.split(du_own, lax.axis_size("ctx"), axis=0)), "ctx", 0, 0),
+        axis=1,
+    )
     long_rows = long_back[0].T.astype(jnp.float32)
     mixer_out = (query_rows * long_rows).astype(jnp.bfloat16)[None]
     grad_prod = du_back[0].T.astype(jnp.float32)

time: 545 us -> 539 us (0.989)
    unnamed x97 -> x156, local copies, waits for them, and re-layouts: 30 us -> 27.5 us
  transfers between devices with their start and end apart: 5 -> 5, of which waited for: 2 -> 2; matrix products, arithmetic and copies ran while one was open for 11% -> 10% of each run, Pallas kernels for 0% -> 0%
where the time goes in v1:
time: 539 us; the launch traced here: 528 us
  local copies, waits for them, and re-layouts  128 us (24%)
  blocking collectives  125 us (23%)
  other arithmetic  116 us (22%)
  waiting for transfers between devices  58.6 us (11%)
  matrix products  52.3 us (10%)
  starting transfers between devices  32.6 us (6%)
  between operations  15.4 us (3%)
    psum x1, blocking collectives, shards(): grad_short = lax.psum(short_terms, ('dp', 'ctx'))  77.5 us
    psum x1, waiting for transfers between devices, shards(): lax.psum(long_terms.astype(jnp.bfloat16), 'dp').astype(jnp.float32)  55.1 us
    dot_general x12, matrix products, matmul(): jnp.dot(left_side, right_side, precision=precise, preferred_element_type=...  52.3 us
    reduce_sum x1, other arithmetic, shards(): jnp.sum(grad_short_out * padded[start:start + row_count], axis=0)  27.9 us
    unnamed x156, local copies, waits for them, and re-layouts  27.5 us
    all_to_all x1, blocking collectives, shards(): lax.all_to_all(jnp.stack(jnp.split(du_own, lax.axis_size('ctx'), axis=0))...  26.8 us
    unnamed x2, other arithmetic  24.3 us
    all_to_all x1, blocking collectives, shards(): lax.all_to_all(product, 'ctx', split_axis=1, concat_axis=0, tiled=True)  21 us
  transfers between devices with their start and end apart: 5, of which 2 were waited for; matrix products, arithmetic and copies ran while one was open for 10% of the time, Pallas kernels for 0%

profile of v1, /device:TPU:1, one launch (start us, length us, event | category | flops | bytes accessed | tf_op | source)
XLA Modules:
  0.0 528.5 jit_solution(18265377582818242935)
XLA Ops:
  8.8 4.5 collective-permute-start
  15.7 4.9 fusion.52
  27.9 11.8 %multiply_add_fusion = f32[128,6144]{0,1:T(8,128)S(1)} fusion(f32[134,6144]{0,1:T(8,128)S(1)} %maximum_convert_fusion, f32[6144]{0:T(1024)S(1)} %broadcast_in_dim.60, f32[6144]{0:T(1024)S(1)} %broadcast_in_dim.58, f32[6144]{0:T(1024)S(1)} %broadcast_in_dim.56, f32[6144]{0:T(1024)S(1)} %broadcast_in_dim.54, f32[6144]{0:T(1024)S(1)} %broadcast_in_dim.52, ...), kind=kLoop, calls=%fused_computation.57 | loop fusion | flops 10223616 | bytes 25337856 | tf_op jit(solution)/shard_map/add | solution.py:120
  41.4 8.1 %copy.2492 = bf16[1,2048,128]{2,0,1:T(2,128)(2,1)S(1)} copy(bf16[1,2048,128]{2,1,0:T(8,128)(2,1)S(1)} %fusion.62) | data formatting | bytes 1048576 | tf_op jit(solution)/shard_map/broadcast_in_dim | solution.py:126
  50.1 12.0 %reduce.18 = bf16[2048,128]{1,0:T(8,128)(2,1)S(1)} reduce(bf16[2048,1,128]{2,1,0:T(2,128)(2,1)S(1)} %bitcast.272, bf16[]{:T(256)} %broadcast.244), dimensions={1}, to_apply=%bitcast.263.reduce_sub_computation | reduce | bytes 1048578
  63.0 13.9 %all-to-all-start.2 = ((bf16[64,2,2048]{2,1,0:T(2,128)(2,1)}), bf16[64,2,2048]{2,1,0:T(2,128)(2,1)S(1)}, u32[]{:S(2)}, u32[]{:S(2)}) async-start(bf16[64,2,2048]{2,1,0:T(2,128)(2,1)} %reshape.242), calls=%async_computation.2 | async-start | bytes 1048576 | tf_op jit(solution)/shard_map/all_to_all | solution.py:134
  76.9 4.7 fusion.131
  94.7 8.8 %bitcast_reduce_fusion.1 = bf16[2048,128]{1,0:T(8,128)(2,1)S(1)} fusion(bf16[2048,1,128]{2,1,0:T(2,128)(2,1)S(1)} %reshape.243), kind=kLoop, calls=%fused_computation.269 | loop fusion | bytes 1048576 | tf_op jit(solution)/shard_map/all_to_all | solution.py:134
  115.5 4.7 multiply_subtract_fusion.4
  129.6 3.7 fusion.16
  136.3 5.6 %copy.2333 = f32[256,32,128]{0,2,1:T(8,128)} copy(f32[256,32,128]{2,0,1:T(8,128)} %pad_maximum_fusion.2) | data formatting | bytes 8388608 | tf_op jit(solution)/shard_map/concatenate | solution.py:75
  141.9 6.2 %fusion.49 = bf16[64,32,128]{2,0,1:T(8,128)(2,1)S(1)} fusion(f32[256,32,128]{0,2,1:T(8,128)} %copy.2333, f32[64,128]{1,0:T(8,128)S(1)} %get-tuple-element.256, f32[64,128]{1,0:T(8,128)S(1)} %get-tuple-element.257), kind=kOutput, calls=%fused_computation.86 | convolution fusion | flops 805601280 | bytes 4784128 | tf_op jit(solution)/shard_map/dot_general | solution.py:23
  150.2 26.8 %all_to_all.32 = bf16[64,1,32,128]{3,2,1,0:T(8,128)(2,1)S(1)} all-to-all(bf16[64,1,32,128]{3,2,1,0:T(8,128)(2,1)S(1)} %constant_dynamic-update-slice_fusion), channel_id=1, replica_groups=mesh['dp'=4,'ctx'=64] {'ctx'}, dimensions={0} | all-to-all | bytes 1048576 | tf_op jit(solution)/shard_map/all_to_all | solution.py:140
  177.3 8.1 %copy.2493 = bf16[1,2048,128]{2,0,1:T(2,128)(2,1)S(1)} copy(bf16[1,2048,128]{2,1,0:T(8,128)(2,1)S(1)} %get-tuple-element.177) | data formatting | bytes 1048576 | tf_op jit(solution)/shard_map/broadcast_in_dim | solution.py:125
  185.4 12.3 %reduce.19 = bf16[2048,128]{1,0:T(8,128)(2,1)} reduce(bf16[2048,1,128]{2,1,0:T(2,128)(2,1)S(1)} %bitcast.273, bf16[]{:T(256)} %broadcast.244), dimensions={1}, to_apply=%bitcast.264.reduce_sub_computation | reduce | bytes 1048578
  198.9 21.0 %all_to_all.33 = bf16[64,2,2048]{2,1,0:T(2,128)(2,1)} all-to-all(bf16[64,2,2048]{2,1,0:T(2,128)(2,1)S(1)} %reshape.244), channel_id=1, replica_groups=mesh['dp'=4,'ctx'=64] {'ctx'}, dimensions={0} | all-to-all | bytes 1048576 | tf_op jit(solution)/shard_map/all_to_all | solution.py:129
  220.0 3.6 reshape.245
  223.6 9.6 %bitcast_reduce_fusion = bf16[2048,128]{1,0:T(8,128)(2,1)} fusion(bf16[2048,1,128]{2,1,0:T(2,128)(2,1)S(1)} %reshape.245), kind=kLoop, calls=%fused_computation.268 | loop fusion | bytes 1048576 | tf_op jit(solution)/shard_map/all_to_all | solution.py:129
  237.9 5.0 fusion
  242.9 6.3 %multiply_subtract_fusion.1 = (f32[128,32,128]{2,0,1:T(8,128)}, f32[128,32,128]{2,0,1:T(8,128)}, f32[128,32,128]{2,0,1:T(8,128)S(1)}, f32[128,32,128]{2,0,1:T(8,128)}) fusion(f32[128,32,256]{2,0,1:T(8,128)S(1)} %copy-done.2, f32[128,32,256]{2,0,1:T(8,128)} %fusion, f32[128,32,256]{2,0,1:T(8,128)S(1)} %copy-done.4), kind=kLoop, calls=%fused_computation.69 | loop fusion | flops 6815744 | bytes 20971520 | tf_op jit(solution)/shard_map/sub | solution.py:98
  249.1 5.7 %fusion.20 = f32[128,32,256]{2,0,1:T(8,128)S(1)} fusion(f32[128,32,128]{2,0,1:T(8,128)} %get-tuple-element.150, f32[128,32,128]{2,0,1:T(8,128)} %get-tuple-element.149, f32[128,128]{1,0:T(8,128)S(1)} %get-tuple-element.253, f32[128,128]{1,0:T(8,128)S(1)} %get-tuple-element.255, f32[128,128]{1,0:T(8,128)S(1)} %get-tuple-element.254), kind=kOutput, calls=%fused_computation.23 | convolution fusion | flops 3222470656 | bytes 8585216 | tf_op jit(solution)/shard_map/dot_general | solution.py:23
  263.7 5.6 %copy.2323 = f32[256,32,128]{0,2,1:T(8,128)} copy(f32[256,32,128]{2,0,1:T(8,128)} %pad_maximum_fusion.1) | data formatting | bytes 8388608 | tf_op jit(solution)/shard_map/concatenate | solution.py:75
  269.3 6.2 %fusion.46 = bf16[64,32,128]{2,0,1:T(8,128)(2,1)S(1)} fusion(f32[256,32,128]{0,2,1:T(8,128)} %copy.2323, f32[64,128]{1,0:T(8,128)S(1)} %copy-done.19, f32[64,128]{1,0:T(8,128)S(1)} %copy-done.21), kind=kOutput, calls=%fused_computation.85 | convolution fusion | flops 805601280 | bytes 4784128 | tf_op jit(solution)/shard_map/dot_general | solution.py:23
  276.7 9.5 %all-to-all-start.1 = ((bf16[64,32,128]{2,1,0:T(8,128)(2,1)}), bf16[64,32,128]{2,1,0:T(8,128)(2,1)}, u32[]{:S(2)}, u32[]{:S(2)}) async-start(bf16[64,32,128]{2,1,0:T(8,128)(2,1)} %copy.2324), calls=%async_computation.1 | async-start | bytes 1048576 | tf_op jit(solution)/shard_map/all_to_all | solution.py:133
  286.2 4.7 pad_maximum_fusion.3
  290.9 6.0 %copy.2336 = f32[256,32,128]{0,2,1:T(8,128)} copy(f32[256,32,128]{2,0,1:T(8,128)} %pad_maximum_fusion.3) | data formatting | bytes 8388608 | tf_op jit(solution)/shard_map/concatenate | solution.py:75
  296.9 6.2 %fusion.43 = bf16[64,32,128]{2,0,1:T(8,128)(2,1)S(1)} fusion(f32[256,32,128]{0,2,1:T(8,128)} %copy.2336, f32[64,128]{1,0:T(8,128)S(1)} %copy-done.19, f32[64,128]{1,0:T(8,128)S(1)} %copy-done.21), kind=kOutput, calls=%fused_computation.84 | convolution fusion | flops 805863424 | bytes 4784128 | tf_op jit(solution)/shard_map/dot_general | solution.py:23
  304.3 55.1 %all-reduce.2.cloned.1.call-done = bf16[32,8192]{1,0:T(8,128)(2,1)} async-done(((bf16[32,8192]{1,0:T(8,128)(2,1)}), bf16[32,8192]{1,0:T(8,128)(2,1)}) %all-reduce.2.cloned.1.call-update) | async-done | bytes 524304 | tf_op jit(solution)/shard_map/psum | solution.py:166
  364.2 27.9 %multiply_reduce_fusion = (f32[6144]{0:T(1024)}, f32[6144]{0:T(1024)}, f32[6144]{0:T(1024)}, f32[6144]{0:T(1024)}, f32[6144]{0:T(1024)}, /*index=5*/f32[6144]{0:T(1024)}, f32[6144]{0:T(1024)}) fusion(f32[134,6144]{0,1:T(8,128)} %copy-done, f32[128,2048]{0,1:T(8,128)S(1)} %get-tuple-element.176, f32[128,2048]{0,1:T(8,128)S(1)} %get-tuple-element.175, ...), kind=kLoop, calls=%fused_computation.50 | loop fusion | flops 12539904 | bytes 25337856 | tf_op jit(solution)/shard_map/reduce_sum | solution.py:162
  408.5 4.6 collective-permute-start.1
  424.2 77.5 %psum.15 = f32[7,768]{1,0:T(8,128)} all-reduce(f32[7,768]{1,0:T(8,128)S(1)} %broadcast_multiply_fusion.1), channel_id=1, replica_groups=mesh['dp'=4,'ctx'=64] {'dp','ctx'}, use_global_device_ids=true, to_apply=%region_9.10 | all-reduce | flops 5376 | bytes 43008 | tf_op jit(solution)/shard_map/psum | solution.py:165
  506.3 12.6 %fusion.39 = bf16[1,128,6144]{1,2,0:T(8,128)(2,1)} fusion(f32[134,6144]{0,1:T(8,128)S(1)} %pad_maximum_fusion, f32[6144]{0:T(1024)S(1)} %copy-done.34, f32[6144]{0:T(1024)S(1)} %copy-done.36, f32[6144]{0:T(1024)S(1)} %copy-done.26, f32[6144]{0:T(1024)S(1)} %copy-done.28, f32[6144]{0:T(1024)S(1)} %copy-done.30, f32[6144]{0:T(1024)S(1)} %copy-done.32, ...), kind=kLoop, calls=%fused_computation.82 | loop fusion | flops 12582912 | bytes 23764992 | tf_op jit(solution)/shard_map/broadcast_in_dim | solution.py:158
  (240 shorter events, 109.9 us)
Async XLA Ops:
  7.2 8.4 %copy-start.13 = (f32[32,8192]{1,0:T(8,128)S(1)}, f32[32,8192]{1,0:T(8,128)}, u32[]{:S(2)}) copy-start(f32[32,8192]{1,0:T(8,128)} %param.6) | copy-start | bytes 3145732
  8.8 14.8 %collective-permute-start = (bf16[6,6144]{1,0:T(8,128)(2,1)}, bf16[6,6144]{1,0:T(8,128)(2,1)S(1)}, u32[]{:S(2)}, u32[]{:S(2)}) collective-permute-start(bf16[6,6144]{1,0:T(8,128)(2,1)} %slice_bitcast_fusion.2), channel_id=1, source_target_pairs={{0,1},{1,2},{2,3},{3,4},{4,5},{5,6},{6,7},{7,8},{8,9},{9,10},{10,1... | collective-permute-start | bytes 221192 | tf_op jit(solution)/shard_map/ppermute | solution.py:13
  15.7 4.9 copy-start.37
  20.7 2.7 copy-start.22
  21.1 6.7 %copy-start.23 = (f32[6144]{0:T(1024)}, f32[6144]{0:T(1024)S(1)}, u32[]{:S(2)}) copy-start(f32[6144]{0:T(1024)S(1)} %broadcast_in_dim.48) | copy-start | bytes 73732
  21.5 6.3 %copy-start.25 = (f32[6144]{0:T(1024)}, f32[6144]{0:T(1024)S(1)}, u32[]{:S(2)}) copy-start(f32[6144]{0:T(1024)S(1)} %broadcast_in_dim.56) | copy-start | bytes 73732
  21.9 5.9 %copy-start.27 = (f32[6144]{0:T(1024)}, f32[6144]{0:T(1024)S(1)}, u32[]{:S(2)}) copy-start(f32[6144]{0:T(1024)S(1)} %broadcast_in_dim.54) | copy-start | bytes 73732
  22.3 5.6 %copy-start.29 = (f32[6144]{0:T(1024)}, f32[6144]{0:T(1024)S(1)}, u32[]{:S(2)}) copy-start(f32[6144]{0:T(1024)S(1)} %broadcast_in_dim.52) | copy-start | bytes 73732
  22.6 5.2 copy-start.31
  23.0 4.8 copy-start.33
  23.4 4.4 copy-start.35
  23.6 16.1 %copy-start.7 = (f32[1,128,2048]{1,2,0:T(8,128)}, f32[1,128,2048]{1,2,0:T(8,128)S(1)}, u32[]{:S(2)}) copy-start(f32[1,128,2048]{1,2,0:T(8,128)S(1)} %copy.2325) | copy-start | bytes 3145732
  27.9 11.9 %copy-start = (f32[134,6144]{0,1:T(8,128)}, f32[134,6144]{0,1:T(8,128)S(1)}, u32[]{:S(2)}) copy-start(f32[134,6144]{0,1:T(8,128)S(1)} %maximum_convert_fusion) | copy-start | bytes 9879556
  63.0 31.2 %all-to-all-start.2 = ((bf16[64,2,2048]{2,1,0:T(2,128)(2,1)}), bf16[64,2,2048]{2,1,0:T(2,128)(2,1)S(1)}, u32[]{:S(2)}, u32[]{:S(2)}) async-start(bf16[64,2,2048]{2,1,0:T(2,128)(2,1)} %reshape.242), calls=%async_computation.2 | async-start | bytes 1048576 | tf_op jit(solution)/shard_map/all_to_all | solution.py:134
  89.4 34.4 %copy-start.9 = (f32[128,128]{1,0:T(8,128)}, f32[128,128]{1,0:T(8,128)S(1)}, u32[]{:S(2)}) copy-start(f32[128,128]{1,0:T(8,128)S(1)} %fusion.113) | copy-start | bytes 196612
  89.7 43.5 %copy-start.14 = (f32[128,128]{1,0:T(8,128)}, f32[128,128]{1,0:T(8,128)S(1)}, u32[]{:S(2)}) copy-start(f32[128,128]{1,0:T(8,128)S(1)} %fusion.102) | copy-start | bytes 196612
  89.9 52.1 %copy-start.18 = (f32[64,128]{1,0:T(8,128)}, f32[64,128]{1,0:T(8,128)S(1)}, u32[]{:S(2)}) copy-start(f32[64,128]{1,0:T(8,128)S(1)} %get-tuple-element.256) | copy-start | bytes 98308
  89.9 52.1 %copy-start.20 = (f32[64,128]{1,0:T(8,128)}, f32[64,128]{1,0:T(8,128)S(1)}, u32[]{:S(2)}) copy-start(f32[64,128]{1,0:T(8,128)S(1)} %get-tuple-element.257) | copy-start | bytes 98308
  90.2 25.4 %copy-start.16 = (f32[128,128]{1,0:T(8,128)}, f32[128,128]{1,0:T(8,128)S(1)}, u32[]{:S(2)}) copy-start(f32[128,128]{1,0:T(8,128)S(1)} %get-tuple-element.251) | copy-start | bytes 196612
  90.7 33.1 %copy-start.11 = (f32[128,128]{1,0:T(8,128)}, f32[128,128]{1,0:T(8,128)S(1)}, u32[]{:S(2)}) copy-start(f32[128,128]{1,0:T(8,128)S(1)} %get-tuple-element.252) | copy-start | bytes 196612
  123.8 3.7 copy-start.1
  148.2 28.9 %copy-start.6 = (f32[128,6144]{0,1:T(8,128)S(1)}, f32[128,6144]{0,1:T(8,128)}, u32[]{:S(2)}) copy-start(f32[128,6144]{0,1:T(8,128)} %copy-done.5) | copy-start | bytes 9437188
  237.9 5.0 copy-start.2
  237.9 5.0 copy-start.4
  249.1 5.7 %copy-start.8 = (f32[128,32,128]{2,0,1:T(8,128)S(1)}, f32[128,32,128]{2,0,1:T(8,128)}, u32[]{:S(2)}) copy-start(f32[128,32,128]{2,0,1:T(8,128)} %get-tuple-element.168) | copy-start | bytes 6291460
  254.8 3.6 copy-start.15
  263.7 5.6 %copy-start.19 = (f32[64,128]{1,0:T(8,128)S(1)}, f32[64,128]{1,0:T(8,128)}, u32[]{:S(2)}) copy-start(f32[64,128]{1,0:T(8,128)} %copy-done.18) | copy-start | bytes 98308
  263.7 5.6 %copy-start.21 = (f32[64,128]{1,0:T(8,128)S(1)}, f32[64,128]{1,0:T(8,128)}, u32[]{:S(2)}) copy-start(f32[64,128]{1,0:T(8,128)} %copy-done.20) | copy-start | bytes 98308
  276.7 84.8 %all-to-all-start.1 = ((bf16[64,32,128]{2,1,0:T(8,128)(2,1)}), bf16[64,32,128]{2,1,0:T(8,128)(2,1)}, u32[]{:S(2)}, u32[]{:S(2)}) async-start(bf16[64,32,128]{2,1,0:T(8,128)(2,1)} %copy.2324), calls=%async_computation.1 | async-start | bytes 1048576 | tf_op jit(solution)/shard_map/all_to_all | solution.py:133
  286.2 73.3 %all-reduce.2.cloned.1.call-start = ((), (), s32[]{:S(2)}) async-start(), calls=%async_computation.4 | async-start | bytes 1048576 | tf_op jit(solution)/shard_map/psum | solution.py:166
  408.5 93.2 %collective-permute-start.1 = (bf16[6,6144]{1,0:T(8,128)(2,1)S(1)}, bf16[6,6144]{1,0:T(8,128)(2,1)S(1)}, u32[]{:S(2)}, u32[]{:S(2)}) collective-permute-start(bf16[6,6144]{1,0:T(8,128)(2,1)S(1)} %copy.2334), channel_id=1, source_target_pairs={{1,0},{2,1},{3,2},{4,3},{5,4},{6,5},{7,6},{8,7},{9,8},{10,9},{11,1... | collective-permute-start | bytes 221192 | tf_op jit(solution)/shard_map/ppermute | solution.py:13
  503.7 2.5 copy-start.32
  (11 other events, 21.2 us)
Sparse Core Ops, SparseCore 0:
  304.4 54.9 all-reduce.1
